TPU v7x, 512 devices: a whole 4x8x8 slice. The times are simulated.
512 devices in a mesh: img: 64 (over z_hi, x, y), tp: 8 (over z_lo, core).
Axes of the slice: x: 4, y: 8, z: 8 (z_hi: 2, z_lo: 4; z = z_hi * 4 + z_lo), core: 2. Of those that a mesh axis runs over, the one named last changes fastest.
Arguments:
- vit_hidden: bfloat16 [8192, 6400], P('img', 'tp'), may hold values from -6 to 6
- residual_stream: bfloat16 [8192, 3200], P('img'), may hold values from -6 to 6
- fc2_weight: bfloat16 [6400, 3200], P('tp', 'img'), may hold values from -0.078125 to 0.078125
- ln_gain: float32 [3200], replicated, may hold values from 0.1 to 1.9
- key_weight: bfloat16 [3200, 2048], P('img', 'tp'), may hold values from -0.109375 to 0.109375
- value_weight: bfloat16 [3200, 2048], P('img', 'tp'), may hold values from -0.109375 to 0.109375
- query_heads: bfloat16 [96, 2048], P(None, 'tp'), may hold values from -64 to 64
- dest_shard: int32 [64], P('img'), may hold values from 0 to 63, as said below
- row_offset: int32 [64], P('img'), may hold values from 0 to 288, as said below
Outputs:
- llm_rows: bfloat16 [24576, 2048], P('img', 'tp')
Inputs may be any that keep to these rules, and one draw needn't show every extreme that they name: `dest_shard`: image slots of one shard never intersect; some shard holds 4 images in every draw. `row_offset`: a multiple of 96.
All inputs are finite; a program needn't handle non-finite values.
Results may differ from a plain program's by a relative error of at most 0.039.
Values may be sent and summed in bfloat16 or wider, within the bound.
A program may use at most 64 MiB of HBM per device.

v0:
```python
import jax
import jax.numpy as jnp
from jax import lax
from jax.sharding import PartitionSpec as P

HEAD_DIM = 128
MOST_IMG = 4


def local(
    vit_hidden,
    residual_stream,
    fc2_weight,
    ln_gain,
    key_weight,
    value_weight,
    query_heads,
    dest_shard,
    row_offset,
):
    act = jax.nn.gelu(vit_hidden.astype(jnp.float32)).astype(jnp.bfloat16)
    partial_out = (
        jnp.dot(
            act,
            lax.all_gather(fc2_weight, "img", axis=1, tiled=True),
            preferred_element_type=jnp.float32,
        )
        .astype(jnp.bfloat16)
        .astype(jnp.float32)
    )
    width = residual_stream.shape[1]
    summed = lax.psum(partial_out.astype(jnp.bfloat16), "tp").astype(jnp.float32)
    stream = residual_stream.astype(jnp.float32) + summed
    mean = jnp.sum(stream, axis=1, keepdims=True) / width
    var = jnp.sum(stream * stream, axis=1, keepdims=True) / width - mean * mean
    normed = ((stream - mean) * lax.rsqrt(var + 1e-06) * ln_gain).astype(jnp.bfloat16)
    cols_kv = key_weight.shape[1]
    keys = jnp.dot(
        normed,
        lax.all_gather(key_weight, "img", axis=0, tiled=True),
        preferred_element_type=jnp.float32,
    )
    values = jnp.dot(
        normed,
        lax.all_gather(value_weight, "img", axis=0, tiled=True),
        preferred_element_type=jnp.float32,
    )
    heads_here = cols_kv // HEAD_DIM
    keys = keys.astype(jnp.bfloat16).reshape(-1, heads_here, HEAD_DIM)
    values = values.astype(jnp.bfloat16).reshape(-1, heads_here, HEAD_DIM)
    queries = query_heads.reshape(-1, heads_here, HEAD_DIM)
    nquery = queries.shape[0]
    scores = jnp.einsum("qhd,phd->hqp", queries, keys, preferred_element_type=jnp.float32) * (
        1.0 / HEAD_DIM**0.5
    )
    peak = jnp.max(scores, axis=2, keepdims=True)
    expo = jnp.exp(scores - peak)
    weights = (expo / jnp.sum(expo, axis=2, keepdims=True)).astype(jnp.bfloat16)
    mixed = jnp.einsum("hqp,phd->qhd", weights, values, preferred_element_type=jnp.float32)
    resampled = mixed.astype(jnp.bfloat16).reshape(nquery, cols_kv)
    me = lax.axis_index("img")
    count = lax.axis_size("img")
    slot_ids = jnp.arange(MOST_IMG, dtype=jnp.int32)
    target = (jnp.arange(count, dtype=jnp.int32) == dest_shard[0])[:, None, None]
    outgoing = jnp.where(target, resampled[None], jnp.zeros((), jnp.bfloat16))
    incoming = lax.all_to_all(outgoing, "img", split_axis=0, concat_axis=0, tiled=True)
    every_dest, every_offset = (
        lax.all_gather(dest_shard, "img", axis=0, tiled=True),
        lax.all_gather(row_offset, "img", axis=0, tiled=True),
    )
    select = (every_dest[None, :] == me) & (every_offset[None, :] // nquery == slot_ids[:, None])
    placed = jnp.dot(
        select.astype(jnp.bfloat16),
        incoming.reshape(count, nquery * cols_kv),
        preferred_element_type=jnp.float32,
    )
    return placed.astype(jnp.bfloat16).reshape(MOST_IMG * nquery, cols_kv)


def solution(mesh):
    return jax.shard_map(
        local,
        mesh=mesh,
        in_specs=(
            P("img", "tp"),
            P("img", None),
            P("tp", "img"),
            P(),
            P("img", "tp"),
            P("img", "tp"),
            P(None, "tp"),
            P("img"),
            P("img"),
        ),
        out_specs=P("img", "tp"),
        check_vma=False,
    )
```

profile of v0, /device:TPU:46, one launch (start us, length us, event | category | flops | bytes accessed | tf_op | source)
XLA Modules:
  0.0 671.4 jit_solution(9044491330760551981)
XLA Ops:
  6.5 0.7 all-gather.7.cloned.1.call-update
  7.3 0.7 all-gather.11.cloned.1.call-update
  8.1 0.7 all-gather.9.cloned.1.call-update
  8.8 185.7 %all-gather.7.cloned.1.call-done = bf16[64,50,800]{2,1,0:T(8,128)(2,1)} async-done(((bf16[1,50,800]{2,1,0:T(8,128)(2,1)}), bf16[64,50,800]{2,1,0:T(8,128)(2,1)}) %all-gather.7.cloned.1.call-update) | async-done | bytes 5120016 | tf_op jit(solution)/shard_map/all_gather | solution.py:25
  194.5 8.7 %reshape.64 = bf16[3200,800]{1,0:T(8,128)(2,1)} reshape(bf16[64,50,800]{2,1,0:T(8,128)(2,1)} %all-gather.7.cloned.1.call-done) | data formatting | bytes 10240000
  203.2 5.4 convolution_convert_fusion.1
  209.3 120.5 %all-gather.11.cloned.1.call-done = bf16[64,50,256]{2,1,0:T(8,128)(2,1)} async-done(((bf16[1,50,256]{2,1,0:T(8,128)(2,1)}), bf16[64,50,256]{2,1,0:T(8,128)(2,1)}) %all-gather.11.cloned.1.call-update) | async-done | bytes 1638416 | tf_op jit(solution)/shard_map/all_gather | solution.py:40
  329.8 2.5 reshape.68
  332.3 132.4 %all-gather.9.cloned.1.call-done = bf16[64,50,256]{2,1,0:T(8,128)(2,1)} async-done(((bf16[1,50,256]{2,1,0:T(8,128)(2,1)}), bf16[64,50,256]{2,1,0:T(8,128)(2,1)}) %all-gather.9.cloned.1.call-update) | async-done | bytes 1638416 | tf_op jit(solution)/shard_map/all_gather | solution.py:45
  464.7 2.5 reshape.66
  467.2 75.1 %all-reduce.5.cloned.1.call-done = bf16[128,3200]{1,0:T(8,128)(2,1)} async-done(((bf16[128,3200]{1,0:T(8,128)(2,1)}), bf16[128,3200]{1,0:T(8,128)(2,1)}) %all-reduce.5.cloned.1.call-update) | async-done | bytes 819216 | tf_op jit(solution)/shard_map/psum | solution.py:32
  542.3 1.9 fusion.1
  544.3 0.5 fusion.6
  545.2 0.5 fusion.5
  545.7 0.4 fusion.7
  546.1 1.9 broadcast_select_fusion
  548.0 13.3 %all-to-all-start = ((bf16[64,96,256]{2,1,0:T(8,128)(2,1)}), bf16[64,96,256]{2,1,0:T(8,128)(2,1)S(1)}, u32[]{:S(2)}, u32[]{:S(2)}) async-start(bf16[64,96,256]{2,1,0:T(8,128)(2,1)} %broadcast_select_fusion), calls=%async_computation | async-start | bytes 6291456 | tf_op jit(solution)/shard_map/all_to_all | solution.py:66
  562.0 1.4 dynamic-slice
  563.3 0.8 dynamic-update-slice
  564.1 0.8 dynamic-update-slice.1
  564.9 96.6 %all-reduce.2 = (s32[64]{0:T(128)S(1)}, s32[64]{0:T(128)S(1)}) all-reduce(s32[64]{0:T(128)S(1)} %dynamic-update-slice.1, s32[64]{0:T(128)S(1)} %dynamic-update-slice), channel_id=1, replica_groups=mesh['img'=64,'tp'=8] {'img'}, use_global_device_ids=true, to_apply=%add.1 | all-reduce | flops 128 | bytes 1024
  661.6 1.9 copy.25
  663.5 0.5 convolution_convert_fusion
  664.0 0.8 reshape.56
  (25 shorter events, 0.6 us)
Async XLA Ops:
  6.5 538.3 %copy-start = (bf16[96,256]{1,0:T(8,128)(2,1)S(1)}, bf16[96,256]{1,0:T(8,128)(2,1)}, u32[]{:S(2)}) copy-start(bf16[96,256]{1,0:T(8,128)(2,1)} %param.15) | copy-start | bytes 147460
  6.5 188.0 %all-gather.7.cloned.1.call-start = ((), (), s32[]{:S(2)}) async-start(), calls=%async_computation.2 | async-start | bytes 6522880 | tf_op jit(solution)/shard_map/all_gather | solution.py:25
  7.3 322.5 %all-gather.11.cloned.1.call-start = ((), (), s32[]{:S(2)}) async-start(), calls=%async_computation.4 | async-start | bytes 1863680 | tf_op jit(solution)/shard_map/all_gather | solution.py:40
  8.0 456.6 %all-gather.9.cloned.1.call-start = ((), (), s32[]{:S(2)}) async-start(), calls=%async_computation.3 | async-start | bytes 1863680 | tf_op jit(solution)/shard_map/all_gather | solution.py:45
  8.7 194.4 %copy-start.3 = (bf16[128,800]{0,1:T(8,128)(2,1)S(1)}, bf16[128,800]{0,1:T(8,128)(2,1)}, u32[]{:S(2)}) copy-start(bf16[128,800]{0,1:T(8,128)(2,1)} %param.9) | copy-start | bytes 614404
  8.8 533.5 %all-reduce.5.cloned.1.call-start = ((), (), s32[]{:S(2)}) async-start(), calls=%async_computation.1 | async-start | bytes 1638400 | tf_op jit(solution)/shard_map/psum | solution.py:32
  464.7 79.6 %copy-start.4 = (f32[3200]{0:T(1024)S(1)}, f32[3200]{0:T(1024)}, u32[]{:S(2)}) copy-start(f32[3200]{0:T(1024)} %param.12) | copy-start | bytes 38404
  542.3 1.9 copy-start.1
  542.3 2.0 copy-start.2
  548.0 113.5 %all-to-all-start = ((bf16[64,96,256]{2,1,0:T(8,128)(2,1)}), bf16[64,96,256]{2,1,0:T(8,128)(2,1)S(1)}, u32[]{:S(2)}, u32[]{:S(2)}) async-start(bf16[64,96,256]{2,1,0:T(8,128)(2,1)} %broadcast_select_fusion), calls=%async_computation | async-start | bytes 6291456 | tf_op jit(solution)/shard_map/all_to_all | solution.py:66
Sparse Core Ops, SparseCore 0:
  11.8 182.6 all-gather.6
  198.9 130.8 all-gather.10
  334.1 130.4 all-gather.8
  467.5 74.7 all-reduce.4
where the time goes:
time: 672 us; the launch traced here: 671 us
  waiting for transfers between devices  516 us (77%)
  blocking collectives  96.6 us (14%)
  local copies, waits for them, and re-layouts  19.4 us (3%)
  between operations  14.6 us (2%)
  starting transfers between devices  13.4 us (2%)
  matrix products  7.54 us (1%)
    all_gather x1, waiting for transfers between devices, local(): lax.all_gather(fc2_weight, 'img', axis=1, tiled=True)  186 us
    all_gather x1, waiting for transfers between devices, local(): lax.all_gather(value_weight, 'img', axis=0, tiled=True)  132 us
    all_gather x1, waiting for transfers between devices, local(): lax.all_gather(key_weight, 'img', axis=0, tiled=True)  120 us
    unnamed x1, blocking collectives  96.6 us
    psum x1, waiting for transfers between devices, local(): lax.psum(partial_out.astype(jnp.bfloat16), 'tp').astype(jnp.float32)  75.1 us
    unnamed x19, local copies, waits for them, and re-layouts  18.6 us
  transfers between devices with their start and end apart: 5, of which 4 were waited for; matrix products, arithmetic and copies ran while one was open for 3% of the time, Pallas kernels for 0%

commit v1 on v0

v1 whole, which is shorter than its diff:
```python
import functools

import jax
import jax.numpy as jnp
from jax import lax
from jax.experimental import pallas as pl
from jax.experimental.pallas import tpu as pltpu
from jax.sharding import PartitionSpec as P

HEAD_DIM = 128
MOST_IMG = 4
ZH, X, Y, ZL, CORES = 2, 4, 8, 4, 2
EPS = 1e-06
MESH = pl.DeviceIdType.MESH
F32 = jnp.float32
BF16 = jnp.bfloat16
COPIES = 96


def window(base, align, span):
    start = lax.div(base, align) * align
    return pl.multiple_of(start, align), base - start


def kernel(
    hidden_ref,
    res_ref,
    w_ref,
    gain_ref,
    kw_ref,
    vw_ref,
    q_ref,
    dest_ref,
    off_ref,
    out_ref,
    act,
    wl,
    kvl,
    own32,
    meta,
    w32,
    kv32,
    res_t,
    res_in,
    resid,
    gain_t,
    part_f,
    part_b,
    part_x,
    half_f,
    half_b,
    half_r,
    stats,
    normed,
    kv_s,
    kv_r,
    rows,
    slab,
    slab_r,
    ss,
    rs,
):
    depth, patches = hidden_ref.shape
    cw = w_ref.shape[0]
    width = res_ref.shape[1]
    kvw = kw_ref.shape[1]
    nquery = q_ref.shape[0]
    heads = kvw // HEAD_DIM
    group = Y * cw

    img = lax.axis_index("img")
    tp = lax.axis_index("tp")
    zh = lax.div(img, X * Y)
    x = lax.rem(lax.div(img, Y), X)
    y = lax.rem(img, Y)
    zl = lax.div(tp, CORES)
    c = lax.rem(tp, CORES)

    def dev(dzh=0, dx=0, dy=0, dzl=0, dc=0):
        a = lax.rem(zh + dzh, ZH)
        b = lax.rem(x + dx + X, X)
        d = lax.rem(y + dy + Y, Y)
        e = lax.rem(zl + dzl + ZL, ZL)
        f = lax.rem(c + dc, CORES)
        return ((a * X + b) * Y + d, e * CORES + f)

    used = [0]
    pending = []

    def copy(src, dst, device):
        n = used[0]
        used[0] += 1
        assert n < COPIES
        return pltpu.make_async_remote_copy(
            src_ref=src,
            dst_ref=dst,
            send_sem=ss.at[n],
            recv_sem=rs.at[n],
            device_id=device,
            device_id_type=MESH,
        )

    def send(src, dst, device):
        cp = copy(src, dst, device)
        cp.start()
        pending.append(cp)
        return cp

    partners = (
        [dev(dzh=1)]
        + [dev(dy=d) for d in range(1, Y)]
        + [dev(dx=d) for d in range(1, X)]
        + [dev(dzl=d) for d in range(1, ZL)]
        + [dev(dc=1)]
        + [dev(dx=d, dzl=-d, dc=k) for d in range(1, X) for k in range(CORES)]
    )
    barrier = pltpu.get_barrier_semaphore()
    for partner in partners:
        pl.semaphore_signal(barrier, inc=1, device_id=partner, device_id_type=MESH)

    own32[0:cw, :] = w_ref[...].astype(F32)
    own32[cw : cw + 1, :] = jnp.full((1, depth), dest_ref[0].astype(F32), F32)
    own32[cw + 1 : cw + 2, :] = jnp.full((1, depth), off_ref[0].astype(F32), F32)
    wl[0, 0] = own32[...].astype(BF16)
    kvl[0, 0, :, 0:kvw] = kw_ref[...]
    kvl[0, 0, :, kvw : 2 * kvw] = vw_ref[...]
    act[0] = jax.nn.gelu(hidden_ref[...].astype(F32)).astype(BF16)
    pl.semaphore_wait(barrier, len(partners))

    w_zh = send(wl.at[0, 0], wl.at[1, 0], dev(dzh=1))
    right, left = {}, {}
    right[0, 1] = send(wl.at[0, 0], wl.at[0, Y - 1], dev(dy=1))
    left[0, 1] = send(wl.at[0, 0], wl.at[0, 1], dev(dy=-1))
    kv_zh = send(kvl.at[0, 0], kvl.at[1, 0], dev(dzh=1))
    act_x = [send(act.at[0], act.at[X - d], dev(dx=d)) for d in range(1, X)]

    owner_x = lax.rem(x - zl + X, X)
    start, shift = window((lax.rem(zh + c, ZH) * X + owner_x) * group, 128, 512)
    res_t[...] = res_ref[:, pl.ds(start, 512)].astype(F32).T.astype(BF16)
    shift = pl.multiple_of(shift, 16)
    res_cp = copy(res_t.at[pl.ds(shift, group)], res_in, dev(dx=-zl))

    @pl.when(zl != 0)
    def _():
        res_cp.start()

    @pl.when(zl == 0)
    def _():
        res_in[...] = res_t[pl.ds(shift, group), :]

    w_zh.wait_recv()
    right[1, 1] = send(wl.at[1, 0], wl.at[1, Y - 1], dev(dy=1))
    left[1, 1] = send(wl.at[1, 0], wl.at[1, 1], dev(dy=-1))

    turn = lax.rem(group - cw * y, group)
    start_g, shift_g = window((lax.rem(zh + c, ZH) * X + x) * group, 128, 512)
    gain_t[...] = jnp.broadcast_to(gain_ref[:, pl.ds(start_g, 512)], (128, 512)).T
    gain_col = pltpu.roll(gain_t[pl.ds(pl.multiple_of(shift_g, 16), group), :], turn, 0)
    gain_t[0:group, :] = gain_col

    def pack(h, r):
        block = wl[h, r].astype(F32)
        w32[h, r * cw : r * cw + cw, :] = block[0:cw, :]
        top = cw // 8 * 8
        meta[h * Y + r, 0 : cw + 2 - top, :] = block[top : cw + 2, 0:kvw]

    pack(0, 0)
    pack(1, 0)
    for s in range(1, Y // 2):
        for h in range(ZH):
            right[h, s].wait_recv()
            if s < Y // 2 - 1 or h == 0:
                right[h, s + 1] = send(wl.at[h, Y - s], wl.at[h, Y - s - 1], dev(dy=1))
            left[h, s].wait_recv()
            if s < Y // 2 - 1 or h == 1:
                left[h, s + 1] = send(wl.at[h, s], wl.at[h, s + 1], dev(dy=-1))
            pack(h, Y - s)
            pack(h, s)
    right[0, Y // 2].wait_recv()
    pack(0, Y // 2)
    left[1, Y // 2].wait_recv()
    pack(1, Y // 2)

    kv_zh.wait_recv()
    kv_y = [
        send(kvl.at[h, 0], kvl.at[h, Y - d], dev(dy=d)) for h in range(ZH) for d in range(1, Y)
    ]

    for cp in act_x:
        cp.wait_recv()
    acts = jnp.concatenate([act[k] for k in range(X)], axis=1)
    for h in range(ZH):
        p = jnp.dot(w32[h].astype(BF16), acts, preferred_element_type=F32)
        part_f[h] = p
        part_b[h] = p.astype(BF16)
    core_cp = send(part_b.at[1 - c], part_x, dev(dc=1))
    core_cp.wait_recv()
    mine = part_f[c] + part_x[...].astype(F32)
    for k in range(X):
        blk = mine[:, k * patches : (k + 1) * patches]
        half_f[k] = blk
        half_b[k] = blk.astype(BF16)
    sums = [
        send(half_b.at[lax.rem(zl + d, ZL)], half_r.at[d - 1], dev(dzl=d)) for d in range(1, ZL)
    ]

    @pl.when(zl != 0)
    def _():
        res_cp.wait_recv()

    resid[...] = pltpu.roll(res_in[...].astype(F32), turn, 0)
    total = half_f[zl] + resid[...]
    for d in range(1, ZL):
        sums[d - 1].wait_recv()
        total = total + half_r[d - 1].astype(F32)

    tall = total.reshape(group // 8, 8, patches)
    stats[0, 0:8] = jnp.sum(tall, axis=0)
    stats[0, 8:16] = jnp.sum(tall * tall, axis=0)
    st = []
    for d in range(X):
        for k in range(CORES):
            if d or k:
                st.append(send(stats.at[0], stats.at[d * CORES + k], dev(dx=d, dzl=-d, dc=k)))
    for cp in st:
        cp.wait_recv()
    both = jnp.sum(stats[...], axis=0)
    mean = jnp.sum(both[0:8], axis=0, keepdims=True) / width
    var = jnp.sum(both[8:16], axis=0, keepdims=True) / width - mean * mean
    normed[c, zl] = ((total - mean) * lax.rsqrt(var + EPS) * gain_t[0:group, :]).astype(BF16)

    ag = [send(normed.at[c, zl], normed.at[c, zl], dev(dzl=d)) for d in range(1, ZL)]
    fw = [send(normed.at[c, zl], normed.at[c, zl], dev(dc=1))]

    for cp in kv_y:
        cp.wait_recv()
    for h in range(ZH):
        for r in range(Y):
            kv32[h, r * cw : r * cw + cw, :] = kvl[h, r].astype(F32)

    for d in range(1, ZL):
        ag[d - 1].wait_recv()
        slot = normed.at[c, lax.rem(zl - d + ZL, ZL)]
        fw.append(send(slot, slot, dev(dc=1)))
    for cp in fw:
        cp.wait_recv()

    acc = None
    for h in range(ZH):
        nt = jnp.concatenate([normed[h, k] for k in range(X)], axis=1)
        p = lax.dot_general(
            kv32[h].astype(BF16), nt, (((0,), (0,)), ((), ())), preferred_element_type=F32
        )
        acc = p if acc is None else acc + p
    for d in range(1, X):
        kv_s[d - 1] = acc[:, d * patches : (d + 1) * patches].astype(BF16)
    kvs = [send(kv_s.at[d - 1], kv_r.at[d - 1], dev(dx=d)) for d in range(1, X)]
    kv = acc[:, 0:patches]
    for d in range(1, X):
        kvs[d - 1].wait_recv()
        kv = kv + kv_r[d - 1].astype(F32)
    kv = kv.astype(BF16)

    for n in range(heads):
        lanes = slice(n * HEAD_DIM, (n + 1) * HEAD_DIM)
        kt = kv[n * HEAD_DIM : (n + 1) * HEAD_DIM, :]
        vt = kv[kvw + n * HEAD_DIM : kvw + (n + 1) * HEAD_DIM, :]
        scores = jnp.dot(q_ref[:, lanes], kt, preferred_element_type=F32) * (1.0 / HEAD_DIM**0.5)
        expo = jnp.exp(scores - jnp.max(scores, axis=1, keepdims=True))
        weights = (expo / jnp.sum(expo, axis=1, keepdims=True)).astype(BF16)
        mixed = lax.dot_general(
            weights, vt, (((1,), (1,)), ((), ())), preferred_element_type=F32
        )
        rows[0, 0, :, lanes] = mixed.astype(BF16)

    r_zh = send(rows.at[0, 0], rows.at[1, 0], dev(dzh=1))
    got = [send(rows.at[0, 0], rows.at[0, Y - d], dev(dy=d)) for d in range(1, Y)]
    r_zh.wait_recv()
    got += [send(rows.at[1, 0], rows.at[1, Y - d], dev(dy=d)) for d in range(1, Y)]
    for cp in got:
        cp.wait_recv()

    skip = cw - cw // 8 * 8
    for k in range(X):
        shard = ((zh * X + lax.rem(x + k, X)) * Y + y).astype(F32)
        for s in range(MOST_IMG):
            picked = None
            for n in range(ZH * Y):
                here = (meta[n, skip : skip + 1, :] == shard) & (
                    meta[n, skip + 1 : skip + 2, :] == float(s * nquery)
                )
                term = rows[n // Y, n % Y] * jnp.where(here, 1.0, 0.0).astype(BF16)
                picked = term if picked is None else picked + term
            slab[k, s * nquery : (s + 1) * nquery, :] = picked
    slabs = [send(slab.at[d], slab_r.at[d - 1], dev(dx=d)) for d in range(1, X)]
    result = slab[0]
    for d in range(1, X):
        slabs[d - 1].wait_recv()
        result = result + slab_r[d - 1]
    out_ref[...] = result

    @pl.when(zl != 0)
    def _():
        res_cp.wait_send()

    for cp in pending:
        cp.wait_send()


def local(
    vit_hidden,
    residual_stream,
    fc2_weight,
    ln_gain,
    key_weight,
    value_weight,
    query_heads,
    dest_shard,
    row_offset,
):
    patches, depth = vit_hidden.shape
    cw = fc2_weight.shape[1]
    kvw = key_weight.shape[1]
    nquery = query_heads.shape[0]
    width = residual_stream.shape[1]
    group = Y * cw
    shard_rows = MOST_IMG * nquery
    vmem = pl.BlockSpec(memory_space=pltpu.VMEM)
    smem = pl.BlockSpec(memory_space=pltpu.SMEM)
    return pl.pallas_call(
        kernel,
        out_shape=jax.ShapeDtypeStruct((shard_rows, kvw), BF16),
        in_specs=[vmem] * 7 + [smem] * 2,
        out_specs=vmem,
        scratch_shapes=[
            pltpu.VMEM((X, depth, patches), BF16),
            pltpu.VMEM((ZH, Y, cw + 2, depth), BF16),
            pltpu.VMEM((ZH, Y, cw, 2 * kvw), BF16),
            pltpu.VMEM((cw + 2, depth), F32),
            pltpu.VMEM((ZH * Y, 8, kvw), F32),
            pltpu.VMEM((ZH, group, depth), F32),
            pltpu.VMEM((ZH, group, 2 * kvw), F32),
            pltpu.VMEM((512, 128), BF16),
            pltpu.VMEM((group, patches), BF16),
            pltpu.VMEM((group, patches), F32),
            pltpu.VMEM((512, 128), F32),
            pltpu.VMEM((ZH, group, X * patches), F32),
            pltpu.VMEM((ZH, group, X * patches), BF16),
            pltpu.VMEM((group, X * patches), BF16),
            pltpu.VMEM((X, group, patches), F32),
            pltpu.VMEM((X, group, patches), BF16),
            pltpu.VMEM((ZL - 1, group, patches), BF16),
            pltpu.VMEM((X * CORES, 16, patches), F32),
            pltpu.VMEM((ZH, X, group, patches), BF16),
            pltpu.VMEM((X - 1, 2 * kvw, patches), BF16),
            pltpu.VMEM((X - 1, 2 * kvw, patches), BF16),
            pltpu.VMEM((ZH, Y, nquery, kvw), BF16),
            pltpu.VMEM((X, shard_rows, kvw), BF16),
            pltpu.VMEM((X - 1, shard_rows, kvw), BF16),
            pltpu.SemaphoreType.DMA((COPIES,)),
            pltpu.SemaphoreType.DMA((COPIES,)),
        ],
        compiler_params=pltpu.CompilerParams(
            collective_id=0, has_side_effects=True, vmem_limit_bytes=48 * 2**20
        ),
        cost_estimate=pl.CostEstimate(
            flops=1100000000, bytes_accessed=3000000, transcendentals=200000
        ),
        name="encoder_resampler",
    )(
        vit_hidden.T,
        residual_stream,
        fc2_weight.T,
        ln_gain.reshape(1, width),
        key_weight,
        value_weight,
        query_heads,
        dest_shard,
        row_offset,
    )


def solution(mesh):
    return jax.shard_map(
        local,
        mesh=mesh,
        in_specs=(
            P("img", "tp"),
            P("img", None),
            P("tp", "img"),
            P(),
            P("img", "tp"),
            P("img", "tp"),
            P(None, "tp"),
            P("img"),
            P("img"),
        ),
        out_specs=P("img", "tp"),
        check_vma=False,
    )
```

time: 672 us -> 123 us (0.18)
  the two profiles are of different devices: /device:TPU:46 before, /device:TPU:192 now
where the time goes in v1:
time: 123 us
  Pallas kernels  115 us (93%)
  local copies, waits for them, and re-layouts  5.92 us (5%)
  between operations  1.34 us (1%)
    pallas_call x1, Pallas kernels, local(): pl.pallas_call(kernel, out_shape=jax.ShapeDtypeStruct((shard_rows, kvw),...  115 us
    unnamed x13, local copies, waits for them, and re-layouts  5.19 us

profile of v1, /device:TPU:192, one launch (start us, length us, event | category | flops | bytes accessed | tf_op | source)
XLA Modules:
  0.0 122.5 jit_solution(213106836436269584)
XLA Ops:
  0.0 0.0 copy-start.4
  1.3 0.7 reshape.3.gain_ref
  2.0 0.0 copy-done.4
  2.0 0.0 copy-start
  2.1 1.1 copy-done
  3.2 0.0 copy-start.1
  3.2 0.9 copy-done.1
  4.1 0.0 copy-start.2
  4.1 0.9 copy-done.2
  5.0 0.0 copy-start.3
  5.0 0.8 copy-done.3
  5.8 0.0 copy-start.5
  5.8 0.7 copy-done.5
  6.6 115.3 %encoder_resampler.1 = bf16[384,256]{1,0:T(8,128)(2,1)S(1)} custom-call(bf16[800,128]{1,0:T(8,128)(2,1)S(1)} %bitcast.2, bf16[128,3200]{1,0:T(8,128)(2,1)S(1)} %copy-done, bf16[50,800]{1,0:T(8,128)(2,1)S(1)} %bitcast.3, f32[1,3200]{1,0:T(1,128)S(1)} %reshape.3.gain_ref, bf16[50,256]{1,0:T(8,128)(2,1)S(1)} %copy-done.4, bf16[50,256]{1,0:T(8,128)(2,1)S(1)} %copy-done.5, ...), custom_call_target="tpu_custom_call" | custom-call | flops 1100000000 | bytes 3000000 | tf_op jit(solution)/shard_map/encoder_resampler/pallas_call | solution.py:330
  121.8 0.7 copy.13
Async XLA Ops:
  0.0 2.0 %copy-start.4 = (bf16[50,256]{1,0:T(8,128)(2,1)S(1)}, bf16[50,256]{1,0:T(8,128)(2,1)}, u32[]{:S(2)}) copy-start(bf16[50,256]{1,0:T(8,128)(2,1)} %kw_ref.1) | copy-start | bytes 76804
  2.0 1.1 copy-start
  3.2 0.9 copy-start.1
  4.1 0.9 copy-start.2
  5.0 0.8 copy-start.3
  5.8 0.7 copy-start.5

commit v2 on v1

v2 whole, which is shorter than its diff:
```python
import functools

import jax
import jax.numpy as jnp
from jax import lax
from jax.experimental import pallas as pl
from jax.experimental.pallas import tpu as pltpu
from jax.sharding import PartitionSpec as P

HEAD_DIM = 128
MOST_IMG = 4
ZH, X, Y, ZL, CORES = 2, 4, 8, 4, 2
EPS = 1e-06
MESH = pl.DeviceIdType.MESH
F32 = jnp.float32
BF16 = jnp.bfloat16
COPIES = 160
ARRIVAL = (0, 1, 7, 2, 6, 3, 5, 4)
FAR_Y = (4, 3, 5, 2, 6, 1, 7)
FAR_X = (2, 1, 3)


def window(base, align):
    start = lax.div(base, align) * align
    return pl.multiple_of(start, align), base - start


def kernel(
    hidden_ref,
    res_ref,
    w_ref,
    gain_ref,
    kw_ref,
    vw_ref,
    q_ref,
    dest_ref,
    off_ref,
    out_ref,
    act,
    wl_a,
    wl_b,
    kvl,
    own32,
    meta,
    w32,
    kv32,
    res_t,
    res_in,
    turned,
    resid,
    gain_t,
    part_f,
    part_b,
    part_x,
    half_f,
    half_b,
    half_r,
    stats,
    normed,
    kv_s,
    kv_r,
    rows,
    slab,
    slab_r,
    ss,
    rs,
    ls,
    hidden_v,
    res_v,
    w_v,
    gain_v,
    q_v,
):
    depth, patches = hidden_ref.shape
    cw = w_ref.shape[0]
    width = res_ref.shape[1]
    kvw = kw_ref.shape[1]
    nquery = q_ref.shape[0]
    heads = kvw // HEAD_DIM
    group = Y * cw

    img = lax.axis_index("img")
    tp = lax.axis_index("tp")
    zh = lax.div(img, X * Y)
    x = lax.rem(lax.div(img, Y), X)
    y = lax.rem(img, Y)
    zl = lax.div(tp, CORES)
    c = lax.rem(tp, CORES)

    def dev(dzh=0, dx=0, dy=0, dzl=0, dc=0):
        a = lax.rem(zh + dzh, ZH)
        b = lax.rem(x + dx + X, X)
        d = lax.rem(y + dy + Y, Y)
        e = lax.rem(zl + dzl + ZL, ZL)
        f = lax.rem(c + dc, CORES)
        return ((a * X + b) * Y + d, e * CORES + f)

    used = [0]
    pending = []

    def arranged(dst, src):
        for p, r in enumerate(ARRIVAL):
            dst[p * cw : (p + 1) * cw, :] = src[r * cw : (r + 1) * cw, :]

    def copy(src, dst, device):
        n = used[0]
        used[0] += 1
        assert n < COPIES
        return pltpu.make_async_remote_copy(
            src_ref=src,
            dst_ref=dst,
            send_sem=ss.at[n],
            recv_sem=rs.at[n],
            device_id=device,
            device_id_type=MESH,
        )

    def send(src, dst, device):
        cp = copy(src, dst, device)
        cp.start()
        pending.append(cp)
        return cp

    partners = (
        [dev(dzh=1)]
        + [dev(dy=d) for d in range(1, Y)]
        + [dev(dx=d) for d in range(1, X)]
        + [dev(dzl=d) for d in range(1, ZL)]
        + [dev(dc=1)]
        + [dev(dx=d, dzl=-d, dc=k) for d in range(1, X) for k in range(CORES)]
    )
    barrier = pltpu.get_barrier_semaphore()
    for partner in partners:
        pl.semaphore_signal(barrier, inc=1, device_id=partner, device_id_type=MESH)

    owner_x = lax.rem(x - zl + X, X)
    start, shift = window((lax.rem(zh + c, ZH) * X + owner_x) * group, 128)
    loads = [
        pltpu.make_async_copy(src, dst, ls.at[n])
        for n, (src, dst) in enumerate(
            (
                (w_ref, w_v),
                (kw_ref, kvl.at[0, 0, :, pl.ds(0, kvw)]),
                (vw_ref, kvl.at[0, 0, :, pl.ds(kvw, kvw)]),
                (hidden_ref, hidden_v),
                (gain_ref, gain_v),
                (res_ref.at[:, pl.ds(start, 512)], res_v),
                (q_ref, q_v),
            )
        )
    ]
    for cp in loads:
        cp.start()

    loads[0].wait()
    own32[0:cw, :] = w_v[...].astype(F32)
    own32[cw : cw + 1, :] = jnp.full((1, depth), dest_ref[0].astype(F32), F32)
    own32[cw + 1 : cw + 2, :] = jnp.full((1, depth), off_ref[0].astype(F32), F32)
    wl = (wl_a, wl_b)
    cut = wl_a.shape[-1]
    wl_a[0, 0] = own32[:, 0:cut].astype(BF16)
    wl_b[0, 0] = own32[:, cut:depth].astype(BF16)
    pl.semaphore_wait(barrier, len(partners))

    w_zh = [send(w.at[0, 0], w.at[1, 0], dev(dzh=1)) for w in wl]
    right, left = {}, {}

    def begin(h, a):
        right[h, a, 1] = send(wl[a].at[h, 0], wl[a].at[h, Y - 1], dev(dy=1))
        left[h, a, 1] = send(wl[a].at[h, 0], wl[a].at[h, 1], dev(dy=-1))

    for a in range(2):
        begin(0, a)
    loads[1].wait()
    loads[2].wait()
    kv_zh = send(kvl.at[0, 0], kvl.at[1, 0], dev(dzh=1))
    loads[3].wait()
    act[0] = jax.nn.gelu(hidden_v[...].astype(F32)).astype(BF16)
    act_x = [send(act.at[0], act.at[X - d], dev(dx=d)) for d in FAR_X]

    loads[5].wait()
    res_t[...] = res_v[...].astype(F32).T.astype(BF16)
    shift = pl.multiple_of(shift, 16)
    res_cp = copy(res_t.at[pl.ds(shift, group)], res_in, dev(dx=-zl))

    @pl.when(zl != 0)
    def _():
        res_cp.start()

    @pl.when(zl == 0)
    def _():
        res_in[...] = res_t[pl.ds(shift, group), :]

    for a in range(2):
        w_zh[a].wait_recv()
        begin(1, a)

    turn = lax.rem(group - cw * y, group)
    start_g, shift_g = window((lax.rem(zh + c, ZH) * X + x) * group, 128)
    loads[4].wait()
    for k in range(4):
        line = gain_v[pl.ds(lax.div(start_g, 128) + k, 1), :]
        gain_t[k * 128 : (k + 1) * 128, :] = jnp.broadcast_to(line, (128, 128)).T
    turned[...] = pltpu.roll(gain_t[pl.ds(pl.multiple_of(shift_g, 16), group), :], turn, 0)
    arranged(gain_t, turned)

    def pack(h, r):
        p = ARRIVAL.index(r)
        block = wl_a[h, r].astype(F32)
        w32[h, p * cw : p * cw + cw, 0:cut] = block[0:cw, :]
        top = cw // 8 * 8
        meta[h * Y + r, 0 : cw + 2 - top, :] = block[top : cw + 2, 0:kvw]
        w32[h, p * cw : p * cw + cw, cut:depth] = wl_b[h, r].astype(F32)[0:cw, :]

    def project(lo, hi):
        acts = jnp.concatenate([act[k] for k in range(X)], axis=1)
        for h in range(ZH):
            p = jnp.dot(w32[h, lo:hi].astype(BF16), acts, preferred_element_type=F32)
            part_f[h, lo:hi] = p
            part_b[h, lo:hi] = p.astype(BF16)
        return send(part_b.at[1 - c, pl.ds(lo, hi - lo)], part_x.at[pl.ds(lo, hi - lo)], dev(dc=1))

    def scatter(lo, hi, core_cp):
        core_cp.wait_recv()
        both = part_f[c, lo:hi] + part_x[lo:hi].astype(F32)
        for k in range(X):
            blk = both[:, k * patches : (k + 1) * patches]
            half_f[k, lo:hi] = blk
            half_b[k, lo:hi] = blk.astype(BF16)
        return [
            send(
                half_b.at[lax.rem(zl + d, ZL), pl.ds(lo, hi - lo)],
                half_r.at[d - 1, pl.ds(lo, hi - lo)],
                dev(dzl=d),
            )
            for d in range(1, ZL)
        ]

    early = 5 * cw // 16 * 16

    def ring(s):
        for h in range(ZH):
            for a in range(2):
                w = wl[a]
                right[h, a, s].wait_recv()
                if s < Y // 2 - 1 or (s < Y // 2 and h == 0):
                    right[h, a, s + 1] = send(w.at[h, Y - s], w.at[h, Y - s - 1], dev(dy=1))
                left[h, a, s].wait_recv()
                if s < Y // 2 - 1 or (s < Y // 2 and h == 1):
                    left[h, a, s + 1] = send(w.at[h, s], w.at[h, s + 1], dev(dy=-1))

    pack(0, 0)
    pack(1, 0)
    ring(1)
    for h in range(ZH):
        pack(h, 1)
        pack(h, Y - 1)
    ring(2)
    for h in range(ZH):
        pack(h, 2)
        pack(h, Y - 2)
    for cp in act_x:
        cp.wait_recv()
    early_cp = project(0, early)
    ring(3)
    early_sums = scatter(0, early, early_cp)
    for h in range(ZH):
        pack(h, 3)
        pack(h, Y - 3)
    for a in range(2):
        right[0, a, Y // 2].wait_recv()
    pack(0, Y // 2)
    for a in range(2):
        left[1, a, Y // 2].wait_recv()
    pack(1, Y // 2)
    late_cp = project(early, group)

    kv_zh.wait_recv()
    kv_y = [send(kvl.at[h, 0], kvl.at[h, Y - d], dev(dy=d)) for h in range(ZH) for d in FAR_Y]

    late_sums = scatter(early, group, late_cp)

    @pl.when(zl != 0)
    def _():
        res_cp.wait_recv()

    turned[...] = pltpu.roll(res_in[...].astype(F32), turn, 0)
    arranged(resid, turned)
    total = half_f[zl] + resid[...]
    for cp in early_sums + late_sums:
        cp.wait_recv()
    for d in range(1, ZL):
        total = total + half_r[d - 1].astype(F32)

    tall = total.reshape(group // 8, 8, patches)
    stats[0, 0:8] = jnp.sum(tall, axis=0)
    stats[0, 8:16] = jnp.sum(tall * tall, axis=0)
    st = []
    for d in range(X):
        for k in range(CORES):
            if d or k:
                st.append(send(stats.at[0], stats.at[d * CORES + k], dev(dx=d, dzl=-d, dc=k)))
    for cp in st:
        cp.wait_recv()
    both = jnp.sum(stats[...], axis=0)
    mean = jnp.sum(both[0:8], axis=0, keepdims=True) / width
    var = jnp.sum(both[8:16], axis=0, keepdims=True) / width - mean * mean
    normed[c, zl] = ((total - mean) * lax.rsqrt(var + EPS) * gain_t[0:group, :]).astype(BF16)

    ag = [send(normed.at[c, zl], normed.at[c, zl], dev(dzl=d)) for d in range(1, ZL)]
    fw = [send(normed.at[c, zl], normed.at[c, zl], dev(dc=1))]

    for cp in kv_y:
        cp.wait_recv()
    for h in range(ZH):
        for r in range(Y):
            p = ARRIVAL.index(r)
            kv32[h, p * cw : p * cw + cw, :] = kvl[h, r].astype(F32)

    for d in range(1, ZL):
        ag[d - 1].wait_recv()
        slot = normed.at[c, lax.rem(zl - d + ZL, ZL)]
        fw.append(send(slot, slot, dev(dc=1)))
    for cp in fw:
        cp.wait_recv()

    acc = None
    for h in range(ZH):
        nt = jnp.concatenate([normed[h, k] for k in range(X)], axis=1)
        p = lax.dot_general(
            kv32[h].astype(BF16), nt, (((0,), (0,)), ((), ())), preferred_element_type=F32
        )
        acc = p if acc is None else acc + p
    for d in range(1, X):
        kv_s[d - 1] = acc[:, d * patches : (d + 1) * patches].astype(BF16)
    kvs = [send(kv_s.at[d - 1], kv_r.at[d - 1], dev(dx=d)) for d in FAR_X]
    kv = acc[:, 0:patches]
    for cp in kvs:
        cp.wait_recv()
    for d in range(1, X):
        kv = kv + kv_r[d - 1].astype(F32)
    kv = kv.astype(BF16)

    loads[6].wait()

    def attend(n):
        kt = kv[n * HEAD_DIM : (n + 1) * HEAD_DIM, :]
        vt = kv[kvw + n * HEAD_DIM : kvw + (n + 1) * HEAD_DIM, :]
        q = q_v[:, n * HEAD_DIM : (n + 1) * HEAD_DIM]
        scores = jnp.dot(q, kt, preferred_element_type=F32) * (1.0 / HEAD_DIM**0.5)
        expo = jnp.exp(scores - jnp.max(scores, axis=1, keepdims=True))
        weights = (expo / jnp.sum(expo, axis=1, keepdims=True)).astype(BF16)
        mixed = lax.dot_general(
            weights, vt, (((1,), (1,)), ((), ())), preferred_element_type=F32
        )
        rows[n, 0, 0] = mixed.astype(BF16)
        return send(rows.at[n, 0, 0], rows.at[n, 1, 0], dev(dzh=1))

    def spread(n, h):
        return {
            d: send(rows.at[n, h, 0], rows.at[n, h, Y - d], dev(dy=d)) for d in (2, Y - 2, 1, Y - 1)
        }

    def relay(n, h, first):
        out = []
        for sign, d in ((1, 2), (-1, Y - 2)):
            first[d].wait_recv()
            slot = (Y - 2 * sign) % Y
            block = rows.at[n, h, slot]
            if sign == (1 if h == 0 else -1):
                out.append(send(block, rows.at[n, h, Y // 2], dev(dy=2 * sign)))
            out.append(send(block, rows.at[n, h, slot - sign], dev(dy=sign)))
        return out + [first[1], first[Y - 1]]

    skip = cw - cw // 8 * 8

    def pick(n):
        for k in range(X):
            shard = ((zh * X + lax.rem(x + k, X)) * Y + y).astype(F32)
            for s in range(MOST_IMG):
                picked = None
                for m in range(ZH * Y):
                    here = (meta[m, skip : skip + 1, 0:HEAD_DIM] == shard) & (
                        meta[m, skip + 1 : skip + 2, 0:HEAD_DIM] == float(s * nquery)
                    )
                    term = rows[n, m // Y, m % Y] * jnp.where(here, 1.0, 0.0).astype(BF16)
                    picked = term if picked is None else picked + term
                slab[n, k, s * nquery : (s + 1) * nquery, :] = picked
        return [send(slab.at[n, d], slab_r.at[n, d - 1], dev(dx=d)) for d in FAR_X]

    r_zh, got, slabs = [], [[] for _ in range(heads)], []
    first = {}
    r_zh.append(attend(0))
    first[0, 0] = spread(0, 0)
    for n in range(1, heads):
        r_zh.append(attend(n))
    for n in range(heads):
        r_zh[n].wait_recv()
        first[n, 1] = spread(n, 1)
        if n + 1 < heads:
            first[n + 1, 0] = spread(n + 1, 0)
        for h in range(ZH):
            got[n] += relay(n, h, first[n, h])
    for n in range(heads):
        for cp in got[n]:
            cp.wait_recv()
        slabs.append(pick(n))
    for n in range(heads):
        for cp in slabs[n]:
            cp.wait_recv()
        result = slab[n, 0]
        for d in range(1, X):
            result = result + slab_r[n, d - 1]
        out_ref[:, n * HEAD_DIM : (n + 1) * HEAD_DIM] = result

    @pl.when(zl != 0)
    def _():
        res_cp.wait_send()

    for cp in pending:
        cp.wait_send()


def local(
    vit_hidden,
    residual_stream,
    fc2_weight,
    ln_gain,
    key_weight,
    value_weight,
    query_heads,
    dest_shard,
    row_offset,
):
    patches, depth = vit_hidden.shape
    cw = fc2_weight.shape[1]
    kvw = key_weight.shape[1]
    nquery = query_heads.shape[0]
    width = residual_stream.shape[1]
    group = Y * cw
    shard_rows = MOST_IMG * nquery
    heads = kvw // HEAD_DIM
    cut = depth // 2 // 128 * 128 + 128
    vmem = pl.BlockSpec(memory_space=pltpu.VMEM)
    smem = pl.BlockSpec(memory_space=pltpu.SMEM)
    return pl.pallas_call(
        kernel,
        out_shape=jax.ShapeDtypeStruct((shard_rows, kvw), BF16),
        in_specs=[pl.BlockSpec(memory_space=pltpu.HBM)] * 7 + [smem] * 2,
        out_specs=vmem,
        scratch_shapes=[
            pltpu.VMEM((X, depth, patches), BF16),
            pltpu.VMEM((ZH, Y, cw + 2, cut), BF16),
            pltpu.VMEM((ZH, Y, cw + 2, depth - cut), BF16),
            pltpu.VMEM((ZH, Y, cw, 2 * kvw), BF16),
            pltpu.VMEM((cw + 2, depth), F32),
            pltpu.VMEM((ZH * Y, 8, kvw), F32),
            pltpu.VMEM((ZH, group, depth), F32),
            pltpu.VMEM((ZH, group, 2 * kvw), F32),
            pltpu.VMEM((512, 128), BF16),
            pltpu.VMEM((group, patches), BF16),
            pltpu.VMEM((group, patches), F32),
            pltpu.VMEM((group, patches), F32),
            pltpu.VMEM((512, 128), F32),
            pltpu.VMEM((ZH, group, X * patches), F32),
            pltpu.VMEM((ZH, group, X * patches), BF16),
            pltpu.VMEM((group, X * patches), BF16),
            pltpu.VMEM((X, group, patches), F32),
            pltpu.VMEM((X, group, patches), BF16),
            pltpu.VMEM((ZL - 1, group, patches), BF16),
            pltpu.VMEM((X * CORES, 16, patches), F32),
            pltpu.VMEM((ZH, X, group, patches), BF16),
            pltpu.VMEM((X - 1, 2 * kvw, patches), BF16),
            pltpu.VMEM((X - 1, 2 * kvw, patches), BF16),
            pltpu.VMEM((heads, ZH, Y, nquery, HEAD_DIM), BF16),
            pltpu.VMEM((heads, X, shard_rows, HEAD_DIM), BF16),
            pltpu.VMEM((heads, X - 1, shard_rows, HEAD_DIM), BF16),
            pltpu.SemaphoreType.DMA((COPIES,)),
            pltpu.SemaphoreType.DMA((COPIES,)),
            pltpu.SemaphoreType.DMA((7,)),
            pltpu.VMEM((depth, patches), BF16),
            pltpu.VMEM((patches, 512), BF16),
            pltpu.VMEM((cw, depth), BF16),
            pltpu.VMEM((width // 128, 128), F32),
            pltpu.VMEM((nquery, kvw), BF16),
        ],
        compiler_params=pltpu.CompilerParams(
            collective_id=0, has_side_effects=True, vmem_limit_bytes=63 * 2**20
        ),
        cost_estimate=pl.CostEstimate(
            flops=1100000000, bytes_accessed=3000000, transcendentals=200000
        ),
        name="encoder_resampler",
    )(
        vit_hidden.T,
        residual_stream,
        fc2_weight.T,
        ln_gain.reshape(width // 128, 128),
        key_weight,
        value_weight,
        query_heads,
        dest_shard,
        row_offset,
    )


def solution(mesh):
    return jax.shard_map(
        local,
        mesh=mesh,
        in_specs=(
            P("img", "tp"),
            P("img", None),
            P("tp", "img"),
            P(),
            P("img", "tp"),
            P("img", "tp"),
            P(None, "tp"),
            P("img"),
            P("img"),
        ),
        out_specs=P("img", "tp"),
        check_vma=False,
    )
```

time: 123 us -> 102 us (0.83)
  the two profiles are of different devices: /device:TPU:192 before, /device:TPU:64 now
where the time goes in v2:
time: 102 us
  Pallas kernels  98.6 us (97%)
  local copies, waits for them, and re-layouts  1.62 us (2%)
  between operations  1.3 us (1%)
    pallas_call x1, Pallas kernels, local(): pl.pallas_call(kernel, out_shape=jax.ShapeDtypeStruct((shard_rows, kvw),...  98.6 us

profile of v2, /device:TPU:64, one launch (start us, length us, event | category | flops | bytes accessed | tf_op | source)
XLA Modules:
  0.0 101.5 jit_solution(7949330726656410779)
XLA Ops:
  1.3 98.6 %encoder_resampler.1 = bf16[384,256]{1,0:T(8,128)(2,1)} custom-call(bf16[800,128]{1,0:T(8,128)(2,1)} %bitcast.3, bf16[128,3200]{1,0:T(8,128)(2,1)} %res_ref.1, bf16[50,800]{1,0:T(8,128)(2,1)} %bitcast.4, f32[25,128]{1,0:T(8,128)} %bitcast.5, bf16[50,256]{1,0:T(8,128)(2,1)} %kw_ref.1, bf16[50,256]{1,0:T(8,128)(2,1)} %vw_ref.1, bf16[96,256]{1,0:T(8,128)(2,1)} %q_ref.1, ...), custom_call_target="tpu_custom_call" | custom-call | flops 1100000000 | bytes 3000000 | tf_op jit(solution)/shard_map/encoder_resampler/pallas_call | solution.py:446
  99.9 1.6 %copy.13 = bf16[384,256]{1,0:T(8,128)(2,1)} copy(bf16[384,256]{1,0:T(8,128)(2,1)} %encoder_resampler.1) | data formatting | bytes 393216

commit v3 on v2

v3 whole, which is shorter than its diff:
```python
import functools

import jax
import jax.numpy as jnp
from jax import lax
from jax.experimental import pallas as pl
from jax.experimental.pallas import tpu as pltpu
from jax.sharding import PartitionSpec as P

HEAD_DIM = 128
MOST_IMG = 4
ZH, X, Y, ZL, CORES = 2, 4, 8, 4, 2
EPS = 1e-06
MESH = pl.DeviceIdType.MESH
F32 = jnp.float32
BF16 = jnp.bfloat16
COPIES = 160
ARRIVAL = (0, 1, 7, 2, 6, 3, 5, 4)
FAR_X = (2, 1, 3)


def window(base, align):
    start = lax.div(base, align) * align
    return pl.multiple_of(start, align), base - start


def kernel(
    hidden_ref,
    res_ref,
    w_ref,
    gain_ref,
    kw_ref,
    vw_ref,
    q_ref,
    dest_ref,
    off_ref,
    out_ref,
    act,
    wl_a,
    wl_b,
    kvl,
    own32,
    meta,
    w32,
    kv32,
    kvt_e,
    kvt_l,
    tilt,
    u_all,
    fin,
    kv_acc,
    res_t,
    res_in,
    turned,
    resid,
    gain_t,
    gain_c,
    part_f,
    part_b,
    part_x,
    half_f,
    half_b,
    half_r,
    stats_e,
    stats_l,
    scale,
    normed,
    kv_own,
    kv_s,
    kv_r,
    rows,
    slab,
    slab_r,
    ss,
    rs,
    ls,
    hidden_v,
    res_v,
    w_v,
    gain_v,
    q_v,
    kw_v,
    vw_v,
    dest_s,
    off_s,
):
    depth, patches = hidden_ref.shape
    cw = w_ref.shape[0]
    width = res_ref.shape[1]
    kvw = kw_ref.shape[1]
    nquery = q_ref.shape[0]
    heads = kvw // HEAD_DIM
    group = Y * cw

    img = lax.axis_index("img")
    tp = lax.axis_index("tp")
    zh = lax.div(img, X * Y)
    x = lax.rem(lax.div(img, Y), X)
    y = lax.rem(img, Y)
    zl = lax.div(tp, CORES)
    c = lax.rem(tp, CORES)

    def dev(dzh=0, dx=0, dy=0, dzl=0, dc=0):
        a = lax.rem(zh + dzh, ZH)
        b = lax.rem(x + dx + X, X)
        d = lax.rem(y + dy + Y, Y)
        e = lax.rem(zl + dzl + ZL, ZL)
        f = lax.rem(c + dc, CORES)
        return ((a * X + b) * Y + d, e * CORES + f)

    used = [0]
    pending = []

    def arranged(dst, src):
        for p, r in enumerate(ARRIVAL):
            dst[p * cw : (p + 1) * cw, :] = src[r * cw : (r + 1) * cw, :]

    def copy(src, dst, device):
        n = used[0]
        used[0] += 1
        assert n < COPIES
        return pltpu.make_async_remote_copy(
            src_ref=src,
            dst_ref=dst,
            send_sem=ss.at[n],
            recv_sem=rs.at[n],
            device_id=device,
            device_id_type=MESH,
        )

    def send(src, dst, device):
        cp = copy(src, dst, device)
        cp.start()
        pending.append(cp)
        return cp

    def spread(ref, h):
        return {d: send(ref.at[h, 0], ref.at[h, Y - d], dev(dy=d)) for d in (2, Y - 2, 1, Y - 1)}

    def relay(ref, h, first):
        out = []
        for sign, d in ((1, 2), (-1, Y - 2)):
            first[d].wait_recv()
            slot = (Y - 2 * sign) % Y
            block = ref.at[h, slot]
            if sign == (1 if h == 0 else -1):
                out.append(send(block, ref.at[h, Y // 2], dev(dy=2 * sign)))
            out.append(send(block, ref.at[h, slot - sign], dev(dy=sign)))
        return out + [first[1], first[Y - 1]]

    partners = (
        [dev(dzh=1)]
        + [dev(dy=d) for d in range(1, Y)]
        + [dev(dx=d) for d in range(1, X)]
        + [dev(dzl=d) for d in range(1, ZL)]
        + [dev(dc=1)]
        + [dev(dx=d, dzl=-d, dc=k) for d in range(1, X) for k in range(CORES)]
        + [dev(dzl=d, dc=1) for d in range(1, ZL)]
    )
    barrier = pltpu.get_barrier_semaphore()
    for partner in partners:
        pl.semaphore_signal(barrier, inc=1, device_id=partner, device_id_type=MESH)

    owner_x = lax.rem(x - zl + X, X)
    start, shift = window((lax.rem(zh + c, ZH) * X + owner_x) * group, 128)
    loads = [
        pltpu.make_async_copy(src, dst, ls.at[n])
        for n, (src, dst) in enumerate(
            (
                (w_ref, w_v),
                (kw_ref, kw_v),
                (vw_ref, vw_v),
                (hidden_ref, hidden_v),
                (gain_ref, gain_v),
                (res_ref.at[:, pl.ds(start, 512)], res_v),
                (q_ref, q_v),
                (dest_ref, dest_s),
                (off_ref, off_s),
            )
        )
    ]
    for cp in loads:
        cp.start()

    tall_rows = own32.shape[0]
    own32[...] = jnp.zeros(own32.shape, F32)
    kvl[0, 0] = jnp.zeros((tall_rows, 2 * kvw), BF16)
    loads[0].wait()
    loads[7].wait()
    loads[8].wait()
    own32[0:cw, 0:depth] = w_v[...].astype(F32)
    own32[cw : cw + 1, 0:depth] = jnp.full((1, depth), dest_s[0].astype(F32), F32)
    own32[cw + 1 : cw + 2, 0:depth] = jnp.full((1, depth), off_s[0].astype(F32), F32)
    wl = (wl_a, wl_b)
    cut = wl_a.shape[-1]
    wl_a[0, 0] = own32[:, 0:cut].astype(BF16)
    wl_b[0, 0] = own32[:, cut:].astype(BF16)
    pl.semaphore_wait(barrier, len(partners))

    w_zh = [send(wl_a.at[0, 0], wl_a.at[1, 0], dev(dzh=1))]
    right, left = {}, {}

    def begin(h, a):
        right[h, a, 1] = send(wl[a].at[h, 0], wl[a].at[h, Y - 1], dev(dy=1))
        left[h, a, 1] = send(wl[a].at[h, 0], wl[a].at[h, 1], dev(dy=-1))

    def sent(*cps):
        for cp in cps:
            cp.wait_send()
            pending[:] = [p for p in pending if p is not cp]

    begin(0, 0)
    loads[1].wait()
    loads[2].wait()
    kvl[0, 0, 0:cw, 0:kvw] = kw_v[...]
    kvl[0, 0, 0:cw, kvw : 2 * kvw] = vw_v[...]
    sent(right[0, 0, 1], left[0, 0, 1])
    begin(0, 1)
    sent(w_zh[0])
    w_zh.append(send(wl_b.at[0, 0], wl_b.at[1, 0], dev(dzh=1)))
    loads[3].wait()
    act[0] = jax.nn.gelu(hidden_v[...].astype(F32)).astype(BF16)
    act_x = [send(act.at[0], act.at[X - d], dev(dx=d)) for d in FAR_X]

    loads[5].wait()
    res_t[...] = res_v[...].astype(F32).T.astype(BF16)
    shift = pl.multiple_of(shift, 16)
    res_cp = copy(res_t.at[pl.ds(shift, group)], res_in, dev(dx=-zl))

    @pl.when(zl != 0)
    def _():
        res_cp.start()

    @pl.when(zl == 0)
    def _():
        res_in[...] = res_t[pl.ds(shift, group), :]

    turn = lax.rem(group - cw * y, group)

    def columns():
        loads[4].wait()
        for h in range(ZH):
            start_g, shift_g = window((lax.rem(zh + h, ZH) * X + x) * group, 128)
            for k in range(4):
                line = gain_v[pl.ds(lax.div(start_g, 128) + k, 1), :]
                gain_t[k * 128 : (k + 1) * 128, :] = jnp.broadcast_to(line, (128, 128)).T
            turned[...] = pltpu.roll(gain_t[pl.ds(pl.multiple_of(shift_g, 16), group), :], turn, 0)
            arranged(gain_c.at[h], turned)

    def pack(h, r):
        p = ARRIVAL.index(r)
        block = wl_a[h, r].astype(F32)
        w32[h, p * cw : p * cw + cw, 0:cut] = block[0:cw, :]
        top = cw // 8 * 8
        meta[h * Y + r] = block[top : top + 8, 0:kvw]
        w32[h, p * cw : p * cw + cw, cut:depth] = wl_b[h, r].astype(F32)[0:cw, 0 : depth - cut]

    def project(lo, hi):
        acts = jnp.concatenate([act[k] for k in range(X)], axis=1)
        for h in range(ZH):
            p = jnp.dot(w32[h, lo:hi].astype(BF16), acts, preferred_element_type=F32)
            part_f[h, lo:hi] = p
            part_b[h, lo:hi] = p.astype(BF16)
        return send(part_b.at[1 - c, pl.ds(lo, hi - lo)], part_x.at[pl.ds(lo, hi - lo)], dev(dc=1))

    def scatter(lo, hi, core_cp):
        core_cp.wait_recv()
        both = part_f[c, lo:hi] + part_x[lo:hi].astype(F32)
        for k in range(X):
            blk = both[:, k * patches : (k + 1) * patches]
            half_f[k, lo:hi] = blk
            half_b[k, lo:hi] = blk.astype(BF16)
        return [
            send(
                half_b.at[lax.rem(zl + d, ZL), pl.ds(lo, hi - lo)],
                half_r.at[d - 1, pl.ds(lo, hi - lo)],
                dev(dzl=d),
            )
            for d in range(1, ZL)
        ]

    early = kvt_e.shape[-1]

    def ring(h, a, s):
        w = wl[a]
        if s < Y // 2 or h == 0:
            right[h, a, s].wait_recv()
        if s < Y // 2 - 1 or (s < Y // 2 and h == 0):
            right[h, a, s + 1] = send(w.at[h, Y - s], w.at[h, Y - s - 1], dev(dy=1))
        if s < Y // 2 or h == 1:
            left[h, a, s].wait_recv()
        if s < Y // 2 - 1 or (s < Y // 2 and h == 1):
            left[h, a, s + 1] = send(w.at[h, s], w.at[h, s + 1], dev(dy=-1))

    def finish(lo, hi, sums, pivot):
        total = half_f[zl, lo:hi] + resid[lo:hi]
        for cp in sums:
            cp.wait_recv()
        for d in range(1, ZL):
            total = total + half_r[d - 1, lo:hi].astype(F32)
        tall = total.reshape((hi - lo) // 8, 8, patches)
        once, twice = jnp.sum(tall, axis=0), jnp.sum(tall * tall, axis=0)
        if pivot is None:
            pivot = jnp.sum(once, axis=0, keepdims=True) / (hi - lo)
        normed[c, zl, lo:hi] = ((total - pivot) * gain_c[c, lo:hi]).astype(BF16)

        def block(k):
            return normed.at[c, k, pl.ds(lo, hi - lo)]

        ag = [send(block(zl), block(zl), dev(dzl=d)) for d in range(1, ZL)]
        fw = [send(block(zl), block(zl), dev(dc=1))]

        def forward(d):
            ag[d - 1].wait_recv()
            k = lax.rem(zl - d + ZL, ZL)
            fw.append(send(block(k), block(k), dev(dc=1)))

        return once, twice, pivot, fw, forward

    def exchange(ref):
        return [
            send(ref.at[0], ref.at[d * CORES + k], dev(dx=d, dzl=-d, dc=k))
            for d in range(X)
            for k in range(CORES)
            if d or k
        ]

    ring(0, 0, 1)
    ring(0, 1, 1)
    ring(0, 0, 2)
    w_zh[0].wait_recv()
    begin(1, 0)
    ring(0, 1, 2)
    w_zh[1].wait_recv()
    begin(1, 1)
    kv_zh = send(kvl.at[0, 0], kvl.at[1, 0], dev(dzh=1))
    columns()
    pack(1, 0)
    for r in (0, 1, Y - 1):
        pack(0, r)
    ring(0, 0, 3)
    ring(1, 0, 1)
    ring(0, 1, 3)
    ring(1, 1, 1)
    for r in (1, Y - 1):
        pack(1, r)
    for cp in act_x:
        cp.wait_recv()
    early_cp = project(0, early)
    ring(0, 0, 4)
    ring(1, 0, 2)
    ring(0, 1, 4)
    ring(1, 1, 2)
    early_sums = scatter(0, early, early_cp)
    for r in (2, Y - 2, 3, Y - 3, 4):
        pack(0, r)
    for r in (2, Y - 2):
        pack(1, r)

    @pl.when(zl != 0)
    def _():
        res_cp.wait_recv()

    turned[...] = pltpu.roll(res_in[...].astype(F32), turn, 0)
    arranged(resid, turned)
    ring(1, 0, 3)
    ring(1, 1, 3)
    once_e, twice_e, here_e, fw_e, forward_e = finish(0, early, early_sums, None)
    stats_e[0] = once_e
    st_e = exchange(stats_e)
    for r in (3, Y - 3):
        pack(1, r)
    ring(1, 0, 4)
    ring(1, 1, 4)
    pack(1, 4)
    late_cp = project(early, group)

    kv_zh.wait_recv()
    kv_first = [spread(kvl, h) for h in range(ZH)]

    late_sums = scatter(early, group, late_cp)
    kv_y = [cp for h in range(ZH) for cp in relay(kvl, h, kv_first[h])]

    for cp in st_e:
        cp.wait_recv()
    sum_e = jnp.sum(jnp.sum(stats_e[...], axis=0), axis=0, keepdims=True)
    pivot = sum_e / (X * CORES * early)
    once_l, twice_l, _, fw_l, forward_l = finish(early, group, late_sums, pivot)
    stats_l[0, 0:8] = once_l
    stats_l[0, 8:16] = twice_e + twice_l
    st_l = exchange(stats_l)
    scale[c, zl] = jnp.broadcast_to(here_e - pivot, (8, patches))
    sc = [
        send(scale.at[c, zl], scale.at[c, zl], dev(dzl=d, dc=k))
        for d in range(ZL)
        for k in range(CORES)
        if d or k
    ]
    for d in range(1, ZL):
        forward_e(d)

    for cp in kv_y:
        cp.wait_recv()
    for h in range(ZH):
        for r in range(Y):
            p = ARRIVAL.index(r)
            kv32[p * cw : p * cw + cw, :] = kvl[h, r].astype(F32)[0:cw, :]
        kvt_e[h] = kv32[0:early].T.astype(BF16)
        kvt_l[h] = kv32[early:group].T.astype(BF16)
        tilt[h] = jnp.dot(
            kvt_e[h], gain_c[h, 0:early].astype(BF16), preferred_element_type=F32
        )
        u = lax.dot_general(
            gain_c[h].astype(BF16),
            kv32[...].astype(BF16),
            (((0,), (0,)), ((), ())),
            preferred_element_type=F32,
        )[0:8]
        weighted = u if h == 0 else weighted + u
    u_all[0] = weighted
    us = [send(u_all.at[0], u_all.at[X - d], dev(dx=d)) for d in FAR_X]

    for cp in fw_e + sc:
        cp.wait_recv()
    acc = None
    for h in range(ZH):
        nt = jnp.concatenate([normed[h, k, 0:early] for k in range(X)], axis=1)
        p = jnp.dot(kvt_e[h], nt, preferred_element_type=F32)
        acc = p if acc is None else acc + p
    for k in range(X):
        part = acc[:, k * patches : (k + 1) * patches]
        for h in range(ZH):
            part = part + tilt[h] * scale[h, k, 0:1, :]
        kv_acc[k] = part
    base = used[0]
    used[0] += X

    def kv_copy(k):
        return pltpu.make_async_remote_copy(
            src_ref=kv_s.at[k],
            dst_ref=kv_r.at[k],
            send_sem=ss.at[base + k],
            recv_sem=rs.at[base + k],
            device_id=dev(dx=k),
            device_id_type=MESH,
        )

    for d in range(ZL):
        k = lax.rem(zl - d + ZL, ZL)
        if d == 1:
            for e in range(1, ZL):
                forward_l(e)
        fw_l[d].wait_recv()
        part = kv_acc[k]
        for h in range(ZH):
            part = part + jnp.dot(
                kvt_l[h], normed[h, k, early:group], preferred_element_type=F32
            )

        @pl.when(k == 0)
        def _():
            kv_own[...] = part

        @pl.when(k != 0)
        def _():
            kv_s[k] = part.astype(BF16)
            kv_copy(k).start()

    for cp in st_l:
        cp.wait_recv()
    fin_cps = [copy(fin, fin, dev(dzl=d)) for d in range(1, ZL)]

    @pl.when(zl == 0)
    def _():
        both = jnp.sum(stats_l[...], axis=0)
        mean = (sum_e + jnp.sum(both[0:8], axis=0, keepdims=True)) / width
        var = jnp.sum(both[8:16], axis=0, keepdims=True) / width - mean * mean
        fin[0:8] = jnp.broadcast_to(lax.rsqrt(var + EPS), (8, patches))
        first_row = lax.broadcasted_iota(jnp.int32, (8, patches), 0) == 0
        fin[8:16] = jnp.where(first_row, jnp.broadcast_to(pivot - mean, (8, patches)), 0.0)
        for cp in fin_cps:
            cp.start()

    for d in range(1, ZL):

        @pl.when(zl == d)
        def _():
            fin_cps[d - 1].wait_recv()

    for cp in us:
        cp.wait_recv()
    kv = kv_own[...] + lax.dot_general(
        jnp.sum(u_all[...], axis=0),
        fin[8:16],
        (((0,), (0,)), ((), ())),
        precision=lax.Precision.HIGHEST,
        preferred_element_type=F32,
    )
    for k in range(1, X):
        kv_copy(k).wait_recv()
    for k in range(1, X):
        kv = kv + kv_r[k].astype(F32)
    kv = (kv * fin[0:1, :]).astype(BF16)

    loads[6].wait()

    def attend(n):
        kt = kv[n * HEAD_DIM : (n + 1) * HEAD_DIM, :]
        vt = kv[kvw + n * HEAD_DIM : kvw + (n + 1) * HEAD_DIM, :]
        q = q_v[:, n * HEAD_DIM : (n + 1) * HEAD_DIM]
        scores = jnp.dot(q, kt, preferred_element_type=F32) * (1.0 / HEAD_DIM**0.5)
        expo = jnp.exp(scores - jnp.max(scores, axis=1, keepdims=True))
        weights = (expo / jnp.sum(expo, axis=1, keepdims=True)).astype(BF16)
        mixed = lax.dot_general(
            weights, vt, (((1,), (1,)), ((), ())), preferred_element_type=F32
        )
        rows[n, 0, 0] = mixed.astype(BF16)
        return send(rows.at[n, 0, 0], rows.at[n, 1, 0], dev(dzh=1))

    skip = cw - cw // 8 * 8

    def pick(n):
        for k in range(X):
            shard = ((zh * X + lax.rem(x + k, X)) * Y + y).astype(F32)
            for s in range(MOST_IMG):
                picked = None
                for m in range(ZH * Y):
                    here = (meta[m, skip : skip + 1, 0:HEAD_DIM] == shard) & (
                        meta[m, skip + 1 : skip + 2, 0:HEAD_DIM] == float(s * nquery)
                    )
                    term = rows[n, m // Y, m % Y] * jnp.where(here, 1.0, 0.0).astype(BF16)
                    picked = term if picked is None else picked + term
                slab[n, k, s * nquery : (s + 1) * nquery, :] = picked
        return [send(slab.at[n, d], slab_r.at[n, d - 1], dev(dx=d)) for d in FAR_X]

    r_zh, got, slabs = [], [[] for _ in range(heads)], []
    first = {}
    r_zh.append(attend(0))
    first[0, 0] = spread(rows.at[0], 0)
    for n in range(1, heads):
        r_zh.append(attend(n))
        first[n, 0] = spread(rows.at[n], 0)
    got[0] += relay(rows.at[0], 0, first[0, 0])
    for n in range(heads):
        r_zh[n].wait_recv()
        first[n, 1] = spread(rows.at[n], 1)
    for n in range(1, heads):
        got[n] += relay(rows.at[n], 0, first[n, 0])
    for n in range(heads):
        got[n] += relay(rows.at[n], 1, first[n, 1])
    for n in range(heads):
        for cp in got[n]:
            cp.wait_recv()
        slabs.append(pick(n))
    for n in range(heads):
        for cp in slabs[n]:
            cp.wait_recv()
        result = slab[n, 0]
        for d in range(1, X):
            result = result + slab_r[n, d - 1]
        out_ref[:, n * HEAD_DIM : (n + 1) * HEAD_DIM] = result

    @pl.when(zl != 0)
    def _():
        res_cp.wait_send()

    @pl.when(zl == 0)
    def _():
        for cp in fin_cps:
            cp.wait_send()

    for k in range(1, X):
        kv_copy(k).wait_send()
    for cp in pending:
        cp.wait_send()


def local(
    vit_hidden,
    residual_stream,
    fc2_weight,
    ln_gain,
    key_weight,
    value_weight,
    query_heads,
    dest_shard,
    row_offset,
):
    patches, depth = vit_hidden.shape
    cw = fc2_weight.shape[1]
    kvw = key_weight.shape[1]
    nquery = query_heads.shape[0]
    width = residual_stream.shape[1]
    group = Y * cw
    shard_rows = MOST_IMG * nquery
    heads = kvw // HEAD_DIM
    early = 3 * cw // 16 * 16
    tall = cw // 8 * 8 + 8
    wide = (depth + 127) // 128 * 128
    cut = depth // 2 // 128 * 128 + 128
    vmem = pl.BlockSpec(memory_space=pltpu.VMEM)
    return pl.pallas_call(
        kernel,
        out_shape=pltpu.VMEM((shard_rows, kvw), BF16),
        in_specs=[pl.BlockSpec(memory_space=pl.ANY)] * 9,
        out_specs=vmem,
        scratch_shapes=[
            pltpu.VMEM((X, depth, patches), BF16),
            pltpu.VMEM((ZH, Y, tall, cut), BF16),
            pltpu.VMEM((ZH, Y, tall, wide - cut), BF16),
            pltpu.VMEM((ZH, Y, tall, 2 * kvw), BF16),
            pltpu.VMEM((tall, wide), F32),
            pltpu.VMEM((ZH * Y, 8, kvw), F32),
            pltpu.VMEM((ZH, group, depth), F32),
            pltpu.VMEM((group, 2 * kvw), F32),
            pltpu.VMEM((ZH, 2 * kvw, early), BF16),
            pltpu.VMEM((ZH, 2 * kvw, group - early), BF16),
            pltpu.VMEM((ZH, 2 * kvw, patches), F32),
            pltpu.VMEM((X, 8, 2 * kvw), F32),
            pltpu.VMEM((16, patches), F32),
            pltpu.VMEM((X, 2 * kvw, patches), F32),
            pltpu.VMEM((512, 128), BF16),
            pltpu.VMEM((group, patches), BF16),
            pltpu.VMEM((group, patches), F32),
            pltpu.VMEM((group, patches), F32),
            pltpu.VMEM((512, 128), F32),
            pltpu.VMEM((ZH, group, 128), F32),
            pltpu.VMEM((ZH, group, X * patches), F32),
            pltpu.VMEM((ZH, group, X * patches), BF16),
            pltpu.VMEM((group, X * patches), BF16),
            pltpu.VMEM((X, group, patches), F32),
            pltpu.VMEM((X, group, patches), BF16),
            pltpu.VMEM((ZL - 1, group, patches), BF16),
            pltpu.VMEM((X * CORES, 8, patches), F32),
            pltpu.VMEM((X * CORES, 16, patches), F32),
            pltpu.VMEM((ZH, X, 8, patches), F32),
            pltpu.VMEM((ZH, X, group, patches), BF16),
            pltpu.VMEM((2 * kvw, patches), F32),
            pltpu.VMEM((X, 2 * kvw, patches), BF16),
            pltpu.VMEM((X, 2 * kvw, patches), BF16),
            pltpu.VMEM((heads, ZH, Y, nquery, HEAD_DIM), BF16),
            pltpu.VMEM((heads, X, shard_rows, HEAD_DIM), BF16),
            pltpu.VMEM((heads, X - 1, shard_rows, HEAD_DIM), BF16),
            pltpu.SemaphoreType.DMA((COPIES,)),
            pltpu.SemaphoreType.DMA((COPIES,)),
            pltpu.SemaphoreType.DMA((9,)),
            pltpu.VMEM((depth, patches), BF16),
            pltpu.VMEM((patches, 512), BF16),
            pltpu.VMEM((cw, depth), BF16),
            pltpu.VMEM((width // 128, 128), F32),
            pltpu.VMEM((nquery, kvw), BF16),
            pltpu.VMEM((cw, kvw), BF16),
            pltpu.VMEM((cw, kvw), BF16),
            pltpu.SMEM((1,), jnp.int32),
            pltpu.SMEM((1,), jnp.int32),
        ],
        compiler_params=pltpu.CompilerParams(
            collective_id=0, has_side_effects=True, vmem_limit_bytes=63 * 2**20
        ),
        cost_estimate=pl.CostEstimate(
            flops=1100000000, bytes_accessed=3000000, transcendentals=200000
        ),
        name="encoder_resampler",
    )(
        vit_hidden.T,
        residual_stream,
        fc2_weight.T,
        ln_gain.reshape(width // 128, 128),
        key_weight,
        value_weight,
        query_heads,
        dest_shard,
        row_offset,
    )


def solution(mesh):
    return jax.shard_map(
        local,
        mesh=mesh,
        in_specs=(
            P("img", "tp"),
            P("img", None),
            P("tp", "img"),
            P(),
            P("img", "tp"),
            P("img", "tp"),
            P(None, "tp"),
            P("img"),
            P("img"),
        ),
        out_specs=P("img", "tp"),
        check_vma=False,
    )
```

time: 102 us -> 98 us (0.961)
  the two profiles are of different devices: /device:TPU:64 before, /device:TPU:2 now
where the time goes in v3:
time: 98 us; the launch traced here: 97.8 us
  Pallas kernels  95.8 us (98%)
  between operations  1.3 us (1%)
    pallas_call x1, Pallas kernels, local(): pl.pallas_call(kernel, out_shape=pltpu.VMEM((shard_rows, kvw), BF16), in_...  95.8 us

profile of v3, /device:TPU:2, one launch (start us, length us, event | category | flops | bytes accessed | tf_op | source)
XLA Modules:
  0.0 97.8 jit_solution(2878074733815426338)
XLA Ops:
  1.3 95.8 %encoder_resampler.1 = bf16[384,256]{1,0:T(8,128)(2,1)S(1)} custom-call(bf16[800,128]{1,0:T(8,128)(2,1)} %bitcast.3, bf16[128,3200]{1,0:T(8,128)(2,1)} %res_ref.1, bf16[50,800]{1,0:T(8,128)(2,1)} %bitcast.4, f32[25,128]{1,0:T(8,128)} %bitcast.5, bf16[50,256]{1,0:T(8,128)(2,1)} %kw_ref.1, bf16[50,256]{1,0:T(8,128)(2,1)} %vw_ref.1, bf16[96,256]{1,0:T(8,128)(2,1)} %q_ref.1, ...), custom_call_target="tpu_custom_call" | custom-call | flops 1100000000 | bytes 3000000 | tf_op jit(solution)/shard_map/encoder_resampler/pallas_call | solution.py:602
  97.2 0.7 copy.11

commit v4 on v3

--- a/solution.py
+++ b/solution.py
@@ -14,7 +14,7 @@
 MESH = pl.DeviceIdType.MESH
 F32 = jnp.float32
 BF16 = jnp.bfloat16
-COPIES = 160
+COPIES = 192
 ARRIVAL = (0, 1, 7, 2, 6, 3, 5, 4)
 FAR_X = (2, 1, 3)
 
@@ -69,6 +69,7 @@
     kv_s,
     kv_r,
     rows,
+    mask,
     slab,
     slab_r,
     ss,
@@ -197,27 +198,19 @@
     wl_b[0, 0] = own32[:, cut:].astype(BF16)
     pl.semaphore_wait(barrier, len(partners))
 
-    w_zh = [send(wl_a.at[0, 0], wl_a.at[1, 0], dev(dzh=1))]
+    w_zh = [send(w.at[0, 0], w.at[1, 0], dev(dzh=1)) for w in wl]
     right, left = {}, {}
 
     def begin(h, a):
         right[h, a, 1] = send(wl[a].at[h, 0], wl[a].at[h, Y - 1], dev(dy=1))
         left[h, a, 1] = send(wl[a].at[h, 0], wl[a].at[h, 1], dev(dy=-1))
 
-    def sent(*cps):
-        for cp in cps:
-            cp.wait_send()
-            pending[:] = [p for p in pending if p is not cp]
-
     begin(0, 0)
+    begin(0, 1)
     loads[1].wait()
     loads[2].wait()
     kvl[0, 0, 0:cw, 0:kvw] = kw_v[...]
     kvl[0, 0, 0:cw, kvw : 2 * kvw] = vw_v[...]
-    sent(right[0, 0, 1], left[0, 0, 1])
-    begin(0, 1)
-    sent(w_zh[0])
-    w_zh.append(send(wl_b.at[0, 0], wl_b.at[1, 0], dev(dzh=1)))
     loads[3].wait()
     act[0] = jax.nn.gelu(hidden_v[...].astype(F32)).astype(BF16)
     act_x = [send(act.at[0], act.at[X - d], dev(dx=d)) for d in FAR_X]
@@ -280,6 +273,7 @@
         ]
 
     early = kvt_e.shape[-1]
+    first_cut = 3 * cw // 16 * 16
 
     def ring(h, a, s):
         w = wl[a]
@@ -346,16 +340,17 @@
         pack(1, r)
     for cp in act_x:
         cp.wait_recv()
-    early_cp = project(0, early)
+    first_cp = project(0, first_cut)
     ring(0, 0, 4)
     ring(1, 0, 2)
     ring(0, 1, 4)
     ring(1, 1, 2)
-    early_sums = scatter(0, early, early_cp)
+    first_sums = scatter(0, first_cut, first_cp)
     for r in (2, Y - 2, 3, Y - 3, 4):
         pack(0, r)
     for r in (2, Y - 2):
         pack(1, r)
+    second_cp = project(first_cut, early)
 
     @pl.when(zl != 0)
     def _():
@@ -365,9 +360,8 @@
     arranged(resid, turned)
     ring(1, 0, 3)
     ring(1, 1, 3)
-    once_e, twice_e, here_e, fw_e, forward_e = finish(0, early, early_sums, None)
-    stats_e[0] = once_e
-    st_e = exchange(stats_e)
+    second_sums = scatter(first_cut, early, second_cp)
+    once_1, twice_1, here_1, fw_1, forward_1 = finish(0, first_cut, first_sums, None)
     for r in (3, Y - 3):
         pack(1, r)
     ring(1, 0, 4)
@@ -378,6 +372,9 @@
     kv_zh.wait_recv()
     kv_first = [spread(kvl, h) for h in range(ZH)]
 
+    once_2, twice_2, here_2, fw_2, forward_2 = finish(first_cut, early, second_sums, None)
+    stats_e[0] = once_1 + once_2
+    st_e = exchange(stats_e)
     late_sums = scatter(early, group, late_cp)
     kv_y = [cp for h in range(ZH) for cp in relay(kvl, h, kv_first[h])]
 
@@ -387,9 +384,10 @@
     pivot = sum_e / (X * CORES * early)
     once_l, twice_l, _, fw_l, forward_l = finish(early, group, late_sums, pivot)
     stats_l[0, 0:8] = once_l
-    stats_l[0, 8:16] = twice_e + twice_l
+    stats_l[0, 8:16] = twice_1 + twice_2 + twice_l
     st_l = exchange(stats_l)
-    scale[c, zl] = jnp.broadcast_to(here_e - pivot, (8, patches))
+    scale[c, zl, 0:8] = jnp.broadcast_to(here_1 - pivot, (8, patches))
+    scale[c, zl, 8:16] = jnp.broadcast_to(here_2 - pivot, (8, patches))
     sc = [
         send(scale.at[c, zl], scale.at[c, zl], dev(dzl=d, dc=k))
         for d in range(ZL)
@@ -397,7 +395,8 @@
         if d or k
     ]
     for d in range(1, ZL):
-        forward_e(d)
+        forward_1(d)
+        forward_2(d)
 
     for cp in kv_y:
         cp.wait_recv()
@@ -407,9 +406,13 @@
             kv32[p * cw : p * cw + cw, :] = kvl[h, r].astype(F32)[0:cw, :]
         kvt_e[h] = kv32[0:early].T.astype(BF16)
         kvt_l[h] = kv32[early:group].T.astype(BF16)
-        tilt[h] = jnp.dot(
-            kvt_e[h], gain_c[h, 0:early].astype(BF16), preferred_element_type=F32
-        )
+        row = lax.broadcasted_iota(jnp.int32, (early, 128), 0)
+        for b, inside in enumerate((row < first_cut, row >= first_cut)):
+            tilt[h, b] = jnp.dot(
+                kvt_e[h],
+                jnp.where(inside, gain_c[h, 0:early], 0.0).astype(BF16),
+                preferred_element_type=F32,
+            )
         u = lax.dot_general(
             gain_c[h].astype(BF16),
             kv32[...].astype(BF16),
@@ -420,7 +423,7 @@
     u_all[0] = weighted
     us = [send(u_all.at[0], u_all.at[X - d], dev(dx=d)) for d in FAR_X]
 
-    for cp in fw_e + sc:
+    for cp in fw_1 + fw_2 + sc:
         cp.wait_recv()
     acc = None
     for h in range(ZH):
@@ -430,7 +433,8 @@
     for k in range(X):
         part = acc[:, k * patches : (k + 1) * patches]
         for h in range(ZH):
-            part = part + tilt[h] * scale[h, k, 0:1, :]
+            for b in range(2):
+                part = part + tilt[h, b] * scale[h, k, 8 * b : 8 * b + 1, :]
         kv_acc[k] = part
     base = used[0]
     used[0] += X
@@ -519,18 +523,28 @@
 
     skip = cw - cw // 8 * 8
 
-    def pick(n):
+    def masks():
         for k in range(X):
             shard = ((zh * X + lax.rem(x + k, X)) * Y + y).astype(F32)
             for s in range(MOST_IMG):
-                picked = None
                 for m in range(ZH * Y):
                     here = (meta[m, skip : skip + 1, 0:HEAD_DIM] == shard) & (
                         meta[m, skip + 1 : skip + 2, 0:HEAD_DIM] == float(s * nquery)
                     )
-                    term = rows[n, m // Y, m % Y] * jnp.where(here, 1.0, 0.0).astype(BF16)
+                    mask[(k * MOST_IMG + s) * ZH * Y + m] = jnp.broadcast_to(
+                        jnp.where(here, 1.0, 0.0), (16, HEAD_DIM)
+                    ).astype(BF16)
+
+    def pick(n):
+        for k in range(X):
+            for s in range(MOST_IMG):
+                picked = None
+                for m in range(ZH * Y):
+                    here = mask[(k * MOST_IMG + s) * ZH * Y + m]
+                    img = rows[n, m // Y, m % Y].reshape(nquery // 16, 16, HEAD_DIM)
+                    term = img * here[None]
                     picked = term if picked is None else picked + term
-                slab[n, k, s * nquery : (s + 1) * nquery, :] = picked
+                slab[n, k, s * nquery : (s + 1) * nquery, :] = picked.reshape(nquery, HEAD_DIM)
         return [send(slab.at[n, d], slab_r.at[n, d - 1], dev(dx=d)) for d in FAR_X]
 
     r_zh, got, slabs = [], [[] for _ in range(heads)], []
@@ -548,6 +562,7 @@
         got[n] += relay(rows.at[n], 0, first[n, 0])
     for n in range(heads):
         got[n] += relay(rows.at[n], 1, first[n, 1])
+    masks()
     for n in range(heads):
         for cp in got[n]:
             cp.wait_recv()
@@ -594,7 +609,7 @@
     group = Y * cw
     shard_rows = MOST_IMG * nquery
     heads = kvw // HEAD_DIM
-    early = 3 * cw // 16 * 16
+    early = 5 * cw // 16 * 16
     tall = cw // 8 * 8 + 8
     wide = (depth + 127) // 128 * 128
     cut = depth // 2 // 128 * 128 + 128
@@ -615,7 +630,7 @@
             pltpu.VMEM((group, 2 * kvw), F32),
             pltpu.VMEM((ZH, 2 * kvw, early), BF16),
             pltpu.VMEM((ZH, 2 * kvw, group - early), BF16),
-            pltpu.VMEM((ZH, 2 * kvw, patches), F32),
+            pltpu.VMEM((ZH, 2, 2 * kvw, patches), F32),
             pltpu.VMEM((X, 8, 2 * kvw), F32),
             pltpu.VMEM((16, patches), F32),
             pltpu.VMEM((X, 2 * kvw, patches), F32),
@@ -633,12 +648,13 @@
             pltpu.VMEM((ZL - 1, group, patches), BF16),
             pltpu.VMEM((X * CORES, 8, patches), F32),
             pltpu.VMEM((X * CORES, 16, patches), F32),
-            pltpu.VMEM((ZH, X, 8, patches), F32),
+            pltpu.VMEM((ZH, X, 16, patches), F32),
             pltpu.VMEM((ZH, X, group, patches), BF16),
             pltpu.VMEM((2 * kvw, patches), F32),
             pltpu.VMEM((X, 2 * kvw, patches), BF16),
             pltpu.VMEM((X, 2 * kvw, patches), BF16),
             pltpu.VMEM((heads, ZH, Y, nquery, HEAD_DIM), BF16),
+            pltpu.VMEM((X * MOST_IMG * ZH * Y, 16, HEAD_DIM), BF16),
             pltpu.VMEM((heads, X, shard_rows, HEAD_DIM), BF16),
             pltpu.VMEM((heads, X - 1, shard_rows, HEAD_DIM), BF16),
             pltpu.SemaphoreType.DMA((COPIES,)),

time: 98 us -> 96 us (0.980)
  the two profiles are of different devices: /device:TPU:2 before, /device:TPU:4 now
where the time goes in v4:
time: 96 us; the launch traced here: 95.9 us
  Pallas kernels  93.9 us (98%)
  between operations  1.3 us (1%)
    pallas_call x1, Pallas kernels, local(): pl.pallas_call(kernel, out_shape=pltpu.VMEM((shard_rows, kvw), BF16), in_...  93.9 us

profile of v4, /device:TPU:4, one launch (start us, length us, event | category | flops | bytes accessed | tf_op | source)
XLA Modules:
  0.0 95.9 jit_solution(18438097878929533651)
XLA Ops:
  1.3 93.9 %encoder_resampler.1 = bf16[384,256]{1,0:T(8,128)(2,1)S(1)} custom-call(bf16[800,128]{1,0:T(8,128)(2,1)} %bitcast.3, bf16[128,3200]{1,0:T(8,128)(2,1)} %res_ref.1, bf16[50,800]{1,0:T(8,128)(2,1)} %bitcast.4, f32[25,128]{1,0:T(8,128)} %bitcast.5, bf16[50,256]{1,0:T(8,128)(2,1)} %kw_ref.1, bf16[50,256]{1,0:T(8,128)(2,1)} %vw_ref.1, bf16[96,256]{1,0:T(8,128)(2,1)} %q_ref.1, ...), custom_call_target="tpu_custom_call" | custom-call | flops 1100000000 | bytes 3000000 | tf_op jit(solution)/shard_map/encoder_resampler/pallas_call | solution.py:617
  95.2 0.7 copy.11
